TPU v7x, 256 devices: a whole 4x4x8 slice. The times are simulated.
256 devices in a mesh: grp: 16 (over y_hi, z), blk: 16 (over x, y_lo, core).
Axes of the slice: x: 4, y: 4 (y_hi: 2, y_lo: 2; y = y_hi * 2 + y_lo), z: 8, core: 2. Of those that a mesh axis runs over, the one named last changes fastest.
Arguments:
- points: float32 [65536, 64], P(('blk', 'grp')), may hold values from -4.6 to 4.6
- lengthscale: float32 [64], replicated, may hold values from 2.56 to 10.16
- noise: float32 [65536], P(('blk', 'grp')), may hold values from 0.01 to 1
- solution: float32 [65536, 32], P(('blk', 'grp')), may hold values from -6 to 6
- residual: float32 [65536, 32], P(('blk', 'grp')), may hold values from -1.2 to 1.2
- direction: float32 [65536, 32], P(('blk', 'grp')), may hold values from -6 to 6
Outputs:
- new_solution: float32 [65536, 32], P(('blk', 'grp'))
- new_residual: float32 [65536, 32], P(('blk', 'grp'))
- new_direction: float32 [65536, 32], P(('blk', 'grp'))
All inputs are finite; a program needn't handle non-finite values.
Results may differ from a plain program's by a relative error of at most 0.009.
Values may be sent and summed in bfloat16 or wider, within the bound.
A program may use at most 64 MiB of HBM per device.

v0:
```python
import jax
import jax.numpy as jnp
from jax import lax
from jax.sharding import PartitionSpec as P


def kernel_tile(rows, rows_sq, cols):
    cols_sq = jnp.sum(jnp.square(cols.astype(jnp.float32)), axis=1)
    cross = jnp.einsum("id,jd->ij", rows, cols, preferred_element_type=jnp.float32)
    dist_sq = rows_sq[:, None] + cols_sq[None, :] - 2.0 * cross
    radius = jnp.sqrt(jnp.maximum(dist_sq, 1e-06))
    shaped = jnp.sqrt(5.0) * radius
    return ((1.0 + shaped + shaped * shaped / 3.0) * jnp.exp(-shaped)).astype(jnp.bfloat16)


def kernel_image(rows, rows_sq, cols, col_dir):
    kern = kernel_tile(rows, rows_sq, cols)
    return jnp.dot(kern, col_dir, preferred_element_type=jnp.float32)


def local(points, lengthscale, noise, solution, residual, direction):
    scaled = (points / lengthscale[None, :]).astype(jnp.bfloat16)
    mine_sq = jnp.sum(jnp.square(scaled.astype(jnp.float32)), axis=1)
    dir_b = direction.astype(jnp.bfloat16)
    group_pts, group_dir = (
        lax.all_gather(scaled, "grp", axis=0, tiled=True),
        lax.all_gather(dir_b, "grp", axis=0, tiled=True),
    )
    product = kernel_image(
        scaled,
        mine_sq,
        lax.all_gather(group_pts, "blk", axis=0, tiled=True),
        lax.all_gather(group_dir, "blk", axis=0, tiled=True),
    )
    image = product + noise[:, None] * direction
    rr = lax.psum(jnp.sum(residual * residual, axis=0), ("grp", "blk"))
    curv = lax.psum(jnp.sum(direction * image, axis=0), ("grp", "blk"))
    alpha = rr / curv
    new_solution = solution + alpha[None, :] * direction
    new_residual = residual - alpha[None, :] * image
    new_rr = lax.psum(jnp.sum(new_residual * new_residual, axis=0), ("grp", "blk"))
    new_direction = new_residual + (new_rr / rr)[None, :] * direction
    return (new_solution, new_residual, new_direction)


def solution(mesh):
    in_specs = (
        P(("blk", "grp"), None),
        P(),
        P(("blk", "grp")),
        P(("blk", "grp"), None),
        P(("blk", "grp"), None),
        P(("blk", "grp"), None),
    )
    out_specs = (P(("blk", "grp"), None), P(("blk", "grp"), None), P(("blk", "grp"), None))
    return jax.shard_map(local, mesh=mesh, in_specs=in_specs, out_specs=out_specs, check_vma=False)
```

profile of v0, /device:TPU:1, one launch (start us, length us, event | category | flops | bytes accessed | tf_op | source)
XLA Modules:
  0.0 356.3 jit_solution(10729005583825524799)
XLA Ops:
  7.2 0.0 copy-start.2
  7.2 0.0 copy-start.4
  7.2 0.0 all-gather.3.cloned.1.call-start
  7.2 0.9 multiply_reduce_fusion.1
  8.2 42.7 %all_gather.12 = bf16[4096,64]{0,1:T(8,128)(2,1)} all-gather(bf16[256,64]{0,1:T(8,128)(2,1)S(1)} %get-tuple-element.8), channel_id=1, replica_groups=mesh['grp'=16,'blk'=16] {'grp'}, dimensions={0}, use_global_device_ids=true | all-gather | bytes 557056 | tf_op jit(solution)/shard_map/all_gather | solution.py:26
  50.9 0.0 all-gather.3.cloned.1.call-update
  50.9 0.0 all-gather.5.cloned.1.call-start
  51.0 0.8 convert_element_type.19
  51.7 33.1 %all_gather.14 = bf16[4096,32]{0,1:T(8,128)(2,1)} all-gather(bf16[256,32]{0,1:T(8,128)(2,1)S(1)} %convert_element_type.19), channel_id=1, replica_groups=mesh['grp'=16,'blk'=16] {'grp'}, dimensions={0}, use_global_device_ids=true | all-gather | bytes 278528 | tf_op jit(solution)/shard_map/all_gather | solution.py:27
  84.8 0.0 all-gather.5.cloned.1.call-update
  84.8 0.9 multiply_reduce_fusion.4
  85.7 24.0 %all-gather.3.cloned.1.call-done = bf16[65536,64]{0,1:T(8,128)(2,1)} async-done(((bf16[4096,64]{0,1:T(8,128)(2,1)}), bf16[65536,64]{0,1:T(8,128)(2,1)}) %all-gather.3.cloned.1.call-update) | async-done | bytes 8388624 | tf_op jit(solution)/shard_map/all_gather | solution.py:32
  109.7 5.5 %multiply_reduce_fusion = f32[65536]{0:T(1024)S(1)} fusion(bf16[65536,64]{0,1:T(8,128)(2,1)} %all-gather.3.cloned.1.call-done), kind=kLoop, calls=%fused_computation.6 | loop fusion | flops 12517376 | bytes 8650752 | tf_op jit(solution)/shard_map/reduce_sum | solution.py:8
  115.2 35.0 %all-gather.5.cloned.1.call-done = bf16[65536,32]{0,1:T(8,128)(2,1)} async-done(((bf16[4096,32]{0,1:T(8,128)(2,1)}), bf16[65536,32]{0,1:T(8,128)(2,1)}) %all-gather.5.cloned.1.call-update) | async-done | bytes 4194320 | tf_op jit(solution)/shard_map/all_gather | solution.py:33
  150.2 0.0 copy-done.2
  150.2 0.0 copy-done.4
  150.2 48.6 %multiply_reduce_fusion.3 = (f32[32]{0:T(128)S(1)}, f32[256,32]{0,1:T(8,128)S(1)}) fusion(f32[256,32]{0,1:T(8,128)S(1)} %copy-done.2, f32[256]{0:T(256)S(1)} %copy-done.4, bf16[65536,32]{0,1:T(8,128)(2,1)} %all-gather.5.cloned.1.call-done, bf16[256,64]{0,1:T(8,128)(2,1)S(1)} %get-tuple-element.8, bf16[65536,64]{0,1:T(8,128)(2,1)} %all-gather.3.cloned.1.call-done, ...), kind=kOutput, calls=%fused_computation.15 | convolution fusion | flops 3422584832 | bytes 12945536 | tf_op jit(solution)/shard_map/dot_general | solution.py:18
  198.8 76.2 %all-reduce = (f32[32]{0:T(128)S(1)}, f32[32]{0:T(128)S(1)}) all-reduce(f32[32]{0:T(128)S(1)} %multiply_reduce_fusion.4, f32[32]{0:T(128)S(1)} %get-tuple-element.11), channel_id=1, replica_groups=mesh['grp'=16,'blk'=16] {'grp','blk'}, use_global_device_ids=true, to_apply=%region_1.0 | all-reduce | flops 64 | bytes 512 | tf_op jit(solution)/shard_map/psum | solution.py:36
  274.9 0.0 copy-done.1
  274.9 0.2 multiply_reduce_fusion.2
  275.1 0.0 copy-start
  275.1 73.6 %psum.23 = f32[32]{0:T(128)S(1)} all-reduce(f32[32]{0:T(128)S(1)} %get-tuple-element.5), channel_id=1, replica_groups=mesh['grp'=16,'blk'=16] {'grp','blk'}, use_global_device_ids=true, to_apply=%region_7.0 | all-reduce | flops 32 | bytes 256 | tf_op jit(solution)/shard_map/psum | solution.py:41
  348.7 0.7 multiply_add_fusion
  349.4 0.0 copy-done
  (5 shorter events, 0.0 us)
Async XLA Ops:
  7.2 143.0 %copy-start.2 = (f32[256,32]{0,1:T(8,128)S(1)}, f32[256,32]{0,1:T(8,128)}, u32[]{:S(2)}) copy-start(f32[256,32]{0,1:T(8,128)} %param.11) | copy-start | bytes 98308
  7.2 143.0 %copy-start.4 = (f32[256]{0:T(256)S(1)}, f32[256]{0:T(256)}, u32[]{:S(2)}) copy-start(f32[256]{0:T(256)} %param.8) | copy-start | bytes 3076
  7.2 102.5 %all-gather.3.cloned.1.call-start = ((), (), s32[]{:S(2)}) async-start(), calls=%async_computation | async-start | bytes 8912896 | tf_op jit(solution)/shard_map/all_gather | solution.py:32
  50.9 99.3 %all-gather.5.cloned.1.call-start = ((), (), s32[]{:S(2)}) async-start(), calls=%async_computation.1 | async-start | bytes 4456448 | tf_op jit(solution)/shard_map/all_gather | solution.py:33
  150.2 124.7 %copy-start.1 = (f32[256,32]{0,1:T(8,128)S(1)}, f32[256,32]{0,1:T(8,128)}, u32[]{:S(2)}) copy-start(f32[256,32]{0,1:T(8,128)} %param.10) | copy-start | bytes 98308
  150.2 198.5 %copy-start.3 = (f32[256,32]{0,1:T(8,128)S(1)}, f32[256,32]{0,1:T(8,128)}, u32[]{:S(2)}) copy-start(f32[256,32]{0,1:T(8,128)} %param.9) | copy-start | bytes 98308
  275.1 74.3 %copy-start = (f32[256,32]{0,1:T(8,128)}, f32[256,32]{0,1:T(8,128)S(1)}, u32[]{:S(2)}) copy-start(f32[256,32]{0,1:T(8,128)S(1)} %get-tuple-element.6) | copy-start | bytes 98308
Sparse Core Ops, SparseCore 0:
  51.0 58.6 all-gather.2
  111.5 38.6 all-gather.4
where the time goes:
time: 357 us; the launch traced here: 356 us
  blocking collectives  226 us (63%)
  waiting for transfers between devices  59.1 us (17%)
  matrix products  48.6 us (14%)
  between operations  14.1 us (4%)
  other arithmetic  8.93 us (3%)
    psum x1, blocking collectives, local(): rr = lax.psum(jnp.sum(residual * residual, axis=0), ('grp', 'blk'))  76.2 us
    psum x1, blocking collectives, local(): lax.psum(jnp.sum(new_residual * new_residual, axis=0), ('grp', 'blk'))  73.6 us
    dot_general x1, matrix products, kernel_image(): return jnp.dot(kern, col_dir, preferred_element_type=jnp.float32)  48.6 us
    all_gather x1, blocking collectives, local(): lax.all_gather(scaled, 'grp', axis=0, tiled=True)  42.7 us
    all_gather x1, waiting for transfers between devices, local(): lax.all_gather(group_dir, 'blk', axis=0, tiled=True)  35 us
    all_gather x1, blocking collectives, local(): lax.all_gather(dir_b, 'grp', axis=0, tiled=True)  33.1 us
    all_gather x1, waiting for transfers between devices, local(): lax.all_gather(group_pts, 'blk', axis=0, tiled=True)  24 us
  transfers between devices with their start and end apart: 2, of which 2 were waited for; matrix products, arithmetic and copies ran while one was open for 2% of the time, Pallas kernels for 0%

commit v1 on v0

v1 whole, which is shorter than its diff:
```python
import functools

import jax
import jax.numpy as jnp
from jax import lax
from jax.experimental import pallas as pl
from jax.experimental.pallas import tpu as pltpu
from jax.sharding import PartitionSpec as P

MESH = pl.DeviceIdType.MESH
F32 = jnp.float32
BF16 = jnp.bfloat16
NT = (((1,), (1,)), ((), ()))

DIM = 64
RHS = 32
BLK = 256
AUG = 16
FEAT = DIM + AUG
PAY = FEAT + RHS
SIDE = 16
PANEL1 = (0, 1, -2, -3)
PANEL2 = (8, -4, -5, 6, 7)
ROWS = PANEL1 + PANEL2
EXPO = -3.2259641843312467
LIN = 1.3416407864998738


def matern(d2):
    d2 = jnp.maximum(d2, 1e-6)
    r = d2 * lax.rsqrt(d2)
    return ((r * (r + LIN) + 0.6) * jnp.exp2(r * EXPO)).astype(BF16)


def place():
    g, b = lax.axis_index("grp"), lax.axis_index("blk")
    p = (g % 8) * 2 + b % 2
    q = (b // 4) * 4 + (g // 8) * 2 + (b // 2) % 2
    return p, q


def device(p, q):
    p, q = lax.rem(p + 32, SIDE), lax.rem(q + 32, SIDE)
    x, y = q // 4, q % 4
    return {"grp": (y // 2) * 8 + p // 2, "blk": x * 4 + (y % 2) * 2 + p % 2}


def kernel(pts, scale, noise, sol, res, direc, out_sol, out_res, out_dir,
           cols, rowpay, rowland, amat, dmat1, dmat2, acc_i, acc_j, ks, ks2, ret, stat, stat2, land1, land2,
           col_sem, row_sem, pay_sem, ret_sem, back_sem, s1_sem, s2_sem, st_sem):
    p, q = place()
    barrier = pltpu.get_barrier_semaphore()

    def greet(k, c):
        pl.semaphore_signal(barrier, inc=1, device_id=device(p + k, q), device_id_type=MESH)
        pl.semaphore_signal(barrier, inc=1, device_id=device(p, q + k), device_id_type=MESH)
        return c

    lax.fori_loop(1, SIDE, greet, 0)

    scaled = (pts[...] / scale[...]).astype(BF16)
    wide = scaled.astype(F32)
    sq = jnp.sum(wide * wide, axis=0, keepdims=True)
    hi = sq.astype(BF16).astype(F32)
    mid = (sq - hi).astype(BF16).astype(F32)
    low = sq - hi - mid
    at = lax.broadcasted_iota(jnp.int32, (AUG, BLK), 0)

    def aug(ones, parts):
        out = jnp.where((at >= ones) & (at < ones + 3), 1.0, 0.0)
        for n, part in enumerate((hi, mid, low)):
            out = jnp.where(at == parts + n, part, out)
        return out.astype(BF16)

    dir_b = direc[...].astype(BF16)
    cols[0, 0:DIM, :] = scaled
    cols[0, DIM:FEAT, :] = aug(0, 3)
    cols[0, FEAT:PAY, :] = dir_b
    rowpay[0:DIM, :] = (wide * -2.0).astype(BF16)
    rowpay[DIM:FEAT, :] = aug(3, 0)
    rowpay[FEAT:PAY, :] = dir_b
    for k in range(SIDE):
        cols[k, PAY:, :] = jnp.zeros((128 - PAY, BLK), BF16)
    acc_i[...] = jnp.zeros_like(acc_i)
    acc_j[...] = jnp.zeros_like(acc_j)

    pl.semaphore_wait(barrier, 2 * (SIDE - 1))

    def send_row(k):
        return pltpu.make_async_remote_copy(
            src_ref=rowpay, dst_ref=rowland.at[k], send_sem=pay_sem, recv_sem=row_sem.at[k],
            device_id=device(p - ROWS[k], q), device_id_type=MESH)

    def send_col(k):
        return pltpu.make_async_remote_copy(
            src_ref=cols.at[0, pl.ds(0, PAY)], dst_ref=cols.at[k, pl.ds(0, PAY)], send_sem=pay_sem,
            recv_sem=col_sem.at[k], device_id=device(p, q - k), device_id_type=MESH)

    def back_row(k):
        return pltpu.make_async_remote_copy(
            src_ref=acc_i.at[k], dst_ref=ret.at[k - 1], send_sem=back_sem, recv_sem=ret_sem,
            device_id=device(p + ROWS[k], q), device_id_type=MESH)

    def back_col(k):
        return pltpu.make_async_remote_copy(
            src_ref=acc_j.at[k], dst_ref=ret.at[k + 7], send_sem=back_sem, recv_sem=ret_sem,
            device_id=device(p, q + k), device_id_type=MESH)

    for k in range(1, 4):
        send_row(k).start()

    def start_col(k, c):
        send_col(k).start()
        return c

    lax.fori_loop(1, SIDE, start_col, 0)
    for k in range(4, 9):
        send_row(k).start()

    def take_row(k, block):
        dmat, first = (dmat1, 0) if k < 4 else (dmat2, 4)
        wide = jnp.concatenate([block[0:FEAT, :], jnp.zeros((128 - FEAT, BLK), BF16)], axis=0)
        amat[k * BLK:(k + 1) * BLK, :] = wide.T
        at = slice((k - first) * BLK, (k - first + 1) * BLK)
        d = block[FEAT:PAY, :]
        dmat[0, :, at] = d
        dmat[1, :, at] = jnp.zeros_like(d) if k == first else d

    take_row(0, rowpay)
    for k in range(1, 4):
        send_row(k).wait_recv()
        take_row(k, rowland.at[k])

    def tile(rows, c):
        a = amat[rows[0] * BLK:(rows[1]) * BLK, :]
        return matern(jnp.dot(a, cols[c], preferred_element_type=F32))

    def give(rows, c, kern):
        c = jnp.int32(c)
        dmat, first = (dmat1, 0) if rows[1] <= 4 else (dmat2, 4)
        half = jnp.where(lax.rem(c, 8) == 0, 1, 0) if rows[0] == first else 0
        d = dmat[half, :, (rows[0] - first) * BLK:(rows[1] - first) * BLK]
        acc_j[c] += jnp.dot(d, kern, preferred_element_type=F32)
        part = lax.dot_general(cols[c, FEAT:PAY, :], kern, NT, preferred_element_type=F32)
        for n, k in enumerate(range(*rows)):
            acc_i[k] += part[:, n * BLK:(n + 1) * BLK]

    def height(rows):
        return (rows[1] - rows[0]) * BLK

    def phase(full, most, waits, backs, before):
        hf, hm = height(full), height(most)
        new = tile(full, 0)
        if before is not None:
            give(*before)
        ks[0:hf, :] = new

        def step(c, rows_new, rows_old, src, dst):
            new = tile(rows_new, c)
            give(rows_old, c - 1, src[0:height(rows_old), :])
            dst[0:height(rows_new), :] = new

        def pair(rows):
            def body(n, carry):
                c = carry
                if waits:
                    send_col(c).wait_recv()
                    send_col(c + 1).wait_recv()
                step(c, rows, rows, *((ks, ks2) if rows == full else (ks2, ks)))
                step(c + 1, rows, rows, *((ks2, ks) if rows == full else (ks, ks2)))
                if backs:
                    @pl.when(c > 1)
                    def _():
                        back_col(c - 1).start()
                    back_col(c).start()
                return c + 2
            return body

        lax.fori_loop(0, 4, pair(full), 1)
        if waits:
            send_col(9).wait_recv()
        step(9, most, full, ks, ks2)
        if backs:
            back_col(8).start()
        lax.fori_loop(0, 3, pair(most), 10)

    phase((0, 4), (1, 4), True, False, None)
    for k in range(4, 9):
        send_row(k).wait_recv()
        take_row(k, rowland.at[k])
    phase((4, 9), (5, 9), False, True, ((1, 4), 15, ks2[0:3 * BLK, :]))
    give((5, 9), 15, ks2[0:4 * BLK, :])
    back_col(15).start()
    for k in range(1, 9):
        back_row(k).start()

    pltpu.make_async_remote_copy(src_ref=ret, dst_ref=ret, send_sem=back_sem, recv_sem=ret_sem,
                                 device_id=device(p + 1, q), device_id_type=MESH).wait_recv()
    total = acc_i[0] + acc_j[0]
    for k in range(23):
        total += ret[k]
    d, r = direc[...], res[...]
    image = total * (5.0 / 3.0) + noise[...] * d
    lane = lax.broadcasted_iota(jnp.int32, (RHS, 128), 1)

    def put(n, v):
        return jnp.where(lane == n, jnp.sum(v, axis=1, keepdims=True), 0.0)

    stat[...] = put(0, r * r) + put(1, d * image) + put(2, r * image) + put(3, image * image)

    def share(src, land, sem, along_p):
        def copy(k):
            to = device(p - k, q) if along_p else device(p, q - k)
            return pltpu.make_async_remote_copy(src_ref=src, dst_ref=land.at[k - 1], send_sem=st_sem,
                                                recv_sem=sem, device_id=to, device_id_type=MESH)

        def start(k, c):
            copy(k).start()
            return c

        lax.fori_loop(1, SIDE, start, 0)
        pltpu.make_async_remote_copy(src_ref=land, dst_ref=land, send_sem=st_sem, recv_sem=sem,
                                     device_id=device(p + 1, q), device_id_type=MESH).wait_recv()
        out = src[...]
        for k in range(SIDE - 1):
            out += land[k]
        return out

    stat2[...] = share(stat, land1, s1_sem, True)
    sums = share(stat2, land2, s2_sem, False)
    rr, curv, rq, qq = (sums[:, n:n + 1] for n in range(4))
    alpha = rr / curv
    new_rr = rr - alpha * (2.0 * rq - alpha * qq)
    beta = new_rr / rr
    out_sol[...] = sol[...] + alpha * d
    new_res = r - alpha * image
    out_res[...] = new_res
    out_dir[...] = new_res + beta * d

    def sent(ref, sem):
        pltpu.make_async_remote_copy(src_ref=ref, dst_ref=ref, send_sem=sem, recv_sem=ret_sem,
                                     device_id=device(p + 1, q), device_id_type=MESH).wait_send()

    sent(rowland.at[pl.ds(1, 8)], pay_sem)
    for k in range(1, SIDE):
        sent(cols.at[k, pl.ds(0, PAY)], pay_sem)
    sent(ret, back_sem)
    sent(land1, st_sem)
    sent(land2, st_sem)


def local(points, lengthscale, noise, solution, residual, direction):
    vmem = pl.BlockSpec(memory_space=pltpu.VMEM)
    out = jax.ShapeDtypeStruct((RHS, BLK), F32)
    dma = pltpu.SemaphoreType.DMA
    new_sol, new_res, new_dir = pl.pallas_call(
        kernel,
        out_shape=(out, out, out),
        in_specs=[vmem] * 6,
        out_specs=(vmem,) * 3,
        scratch_shapes=[
            pltpu.VMEM((SIDE, 128, BLK), BF16),
            pltpu.VMEM((PAY, BLK), BF16),
            pltpu.VMEM((9, PAY, BLK), BF16),
            pltpu.VMEM((9 * BLK, 128), BF16),
            pltpu.VMEM((2, RHS, 4 * BLK), BF16),
            pltpu.VMEM((2, RHS, 5 * BLK), BF16),
            pltpu.VMEM((9, RHS, BLK), F32),
            pltpu.VMEM((SIDE, RHS, BLK), F32),
            pltpu.VMEM((5 * BLK, BLK), BF16),
            pltpu.VMEM((5 * BLK, BLK), BF16),
            pltpu.VMEM((23, RHS, BLK), F32),
            pltpu.VMEM((RHS, 128), F32),
            pltpu.VMEM((RHS, 128), F32),
            pltpu.VMEM((SIDE - 1, RHS, 128), F32),
            pltpu.VMEM((SIDE - 1, RHS, 128), F32),
            dma((SIDE,)),
            dma((9,)),
            dma,
            dma,
            dma,
            dma,
            dma,
            dma,
        ],
        compiler_params=pltpu.CompilerParams(
            collective_id=0, has_side_effects=True, vmem_limit_bytes=40 * 2**20),
        name="cg_step",
    )(points.T, lengthscale[:, None], noise[None, :], solution.T, residual.T, direction.T)
    return new_sol.T, new_res.T, new_dir.T


def solution(mesh):
    rows = P(("blk", "grp"), None)
    in_specs = (rows, P(), P(("blk", "grp")), rows, rows, rows)
    return jax.shard_map(local, mesh=mesh, in_specs=in_specs, out_specs=(rows,) * 3, check_vma=False)
```

time: 357 us -> 66.9 us (0.19)
  blocking collectives: 226 us -> 0 us
  Pallas kernels: 0 us -> 60.2 us
  waiting for transfers between devices: 59.1 us -> 0 us
  matrix products: 48.6 us -> 0 us
  between operations: 14.1 us -> 0.67 us
  other arithmetic: 8.93 us -> 0 us
  local copies, waits for them, and re-layouts: 0.02 us -> 4.96 us
    psum x2 -> x0, blocking collectives: 150 us -> none  [the longest x1 76.2 us: local(): rr = lax.psum(jnp.sum(residual * residual, axis=0), ('grp', 'blk'))]
    all_gather x2 -> x0, blocking collectives: 75.8 us -> none  [the longest x1 42.7 us: local(): lax.all_gather(scaled, 'grp', axis=0, tiled=True)]
    pallas_call x0 -> x1, Pallas kernels: none -> 60.2 us  [local(): pl.pallas_call(kernel, out_shape=(out, out, out), in_specs=[vmem] * 6, ou...]
    all_gather x2 -> x0, waiting for transfers between devices: 59 us -> none  [the longest x1 35 us: local(): lax.all_gather(group_dir, 'blk', axis=0, tiled=True)]
    dot_general x1 -> x0, matrix products: 48.6 us -> none  [kernel_image(): return jnp.dot(kern, col_dir, preferred_element_type=jnp.float32)]
    reduce_sum x4 -> x0, other arithmetic: 7.45 us -> none  [the longest x1 5.46 us: kernel_tile(): cols_sq = jnp.sum(jnp.square(cols.astype(jnp.float32)), axis=1)]
    unnamed x10 -> x13, local copies, waits for them, and re-layouts: 0.02 us -> 4.2 us
  transfers between devices with their start and end apart: 2 -> 0, of which waited for: 2 -> 0; matrix products, arithmetic and copies ran while one was open for 2% -> 0% of each run, Pallas kernels for 0% -> 0%
where the time goes in v1:
time: 66.9 us; the launch traced here: 65.9 us
  Pallas kernels  60.2 us (90%)
  local copies, waits for them, and re-layouts  4.96 us (7%)
  between operations  0.67 us (1%)
    pallas_call x1, Pallas kernels, local(): pl.pallas_call(kernel, out_shape=(out, out, out), in_specs=[vmem] * 6, ou...  60.2 us
    unnamed x13, local copies, waits for them, and re-layouts  4.2 us

profile of v1, /device:TPU:1, one launch (start us, length us, event | category | flops | bytes accessed | tf_op | source)
XLA Modules:
  0.0 65.9 jit_solution(2935310996900405164)
XLA Ops:
  0.6 0.0 copy-start.1
  0.6 0.0 copy-start.4
  0.7 0.8 %copy.9.scale = f32[64,1]{1,0:T(8,128)S(1)} copy(f32[64,1]{0,1:T(1,128)} %bitcast.17) | data formatting | bytes 512 | tf_op jit(solution)/shard_map/broadcast_in_dim | solution.py:289
  1.4 0.0 copy-done.1
  1.4 0.0 copy-done.4
  1.4 0.0 copy-start
  1.4 0.8 %copy-done = f32[256,64]{0,1:T(8,128)S(1)} copy-done((f32[256,64]{0,1:T(8,128)S(1)}, f32[256,64]{0,1:T(8,128)}, u32[]{:S(2)}) %copy-start) | copy-done | bytes 65560
  2.3 0.0 copy-start.2
  2.3 0.8 %copy-done.2 = f32[256,32]{0,1:T(8,128)S(1)} copy-done((f32[256,32]{0,1:T(8,128)S(1)}, f32[256,32]{0,1:T(8,128)}, u32[]{:S(2)}) %copy-start.2) | copy-done | bytes 32792
  3.0 0.0 copy-start.3
  3.0 0.8 %copy-done.3 = f32[256,32]{0,1:T(8,128)S(1)} copy-done((f32[256,32]{0,1:T(8,128)S(1)}, f32[256,32]{0,1:T(8,128)}, u32[]{:S(2)}) %copy-start.3) | copy-done | bytes 32792
  3.8 60.2 %cg_step.1 = (f32[32,256]{1,0:T(8,128)S(1)}, f32[32,256]{1,0:T(8,128)S(1)}, f32[32,256]{1,0:T(8,128)S(1)}) custom-call(f32[64,256]{1,0:T(8,128)S(1)} %bitcast.9, f32[64,1]{1,0:T(8,128)S(1)} %copy.9.scale, f32[1,256]{1,0:T(1,128)S(1)} %bitcast.16, f32[32,256]{1,0:T(8,128)S(1)} %bitcast.13, f32[32,256]{1,0:T(8,128)S(1)} %bitcast.14, f32[32,256]{1,0:T(8,128)S(1)} %bitcast.15), custom_call_target="tpu_custom_call" | custom-call | tf_op jit(solution)/shard_map/cg_step/pallas_call | solution.py:256
  64.0 0.6 copy.13
  64.6 0.6 copy.14
  65.2 0.6 copy.15
Async XLA Ops:
  0.6 0.8 %copy-start.1 = (f32[256,32]{0,1:T(8,128)S(1)}, f32[256,32]{0,1:T(8,128)}, u32[]{:S(2)}) copy-start(f32[256,32]{0,1:T(8,128)} %param.9) | copy-start | bytes 98308
  0.6 0.8 %copy-start.4 = (f32[256]{0:T(256)S(1)}, f32[256]{0:T(256)}, u32[]{:S(2)}) copy-start(f32[256]{0:T(256)} %param.8) | copy-start | bytes 3076
  1.4 0.8 %copy-start = (f32[256,64]{0,1:T(8,128)S(1)}, f32[256,64]{0,1:T(8,128)}, u32[]{:S(2)}) copy-start(f32[256,64]{0,1:T(8,128)} %param.6) | copy-start | bytes 196612
  2.3 0.8 %copy-start.2 = (f32[256,32]{0,1:T(8,128)S(1)}, f32[256,32]{0,1:T(8,128)}, u32[]{:S(2)}) copy-start(f32[256,32]{0,1:T(8,128)} %param.10) | copy-start | bytes 98308
  3.0 0.8 %copy-start.3 = (f32[256,32]{0,1:T(8,128)S(1)}, f32[256,32]{0,1:T(8,128)}, u32[]{:S(2)}) copy-start(f32[256,32]{0,1:T(8,128)} %param.11) | copy-start | bytes 98308

commit v2 on v1

v2 whole, which is shorter than its diff:
```python
import jax
import jax.numpy as jnp
from jax import lax
from jax.experimental import pallas as pl
from jax.experimental.pallas import tpu as pltpu
from jax.sharding import PartitionSpec as P

MESH = pl.DeviceIdType.MESH
F32 = jnp.float32
BF16 = jnp.bfloat16
NT = (((1,), (1,)), ((), ()))

DIM = 64
RHS = 32
BLK = 256
AUG = 16
FEAT = DIM + AUG
PAY = FEAT + RHS
SIDE = 16
PANEL1 = (0, 1, -4, 3)
PANEL2 = (8, -5, 2, 6, -7)
ROWS = PANEL1 + PANEL2
F1, M1 = (0, 4), (1, 4)
F2, M2 = (4, 9), (5, 9)
EXPO = -3.2259641843312467
LIN = 1.3416407864998738


def matern(d2):
    d2 = jnp.maximum(d2, 1e-6)
    r = d2 * lax.rsqrt(d2)
    return ((r * (r + LIN) + 0.6) * jnp.exp2(r * EXPO)).astype(BF16)


def place():
    g, b = lax.axis_index("grp"), lax.axis_index("blk")
    return (b // 4) * 4 + (g // 8) * 2 + (b // 2) % 2, (g % 8) * 2 + b % 2


def device(p, q):
    p, q = lax.rem(p + 32, SIDE), lax.rem(q + 32, SIDE)
    x, y = p // 4, p % 4
    return {"grp": (y // 2) * 8 + q // 2, "blk": x * 4 + (y % 2) * 2 + q % 2}


def slot(k):
    return lax.rem(k + 32, SIDE)


def kernel(pts_hbm, scale_hbm, noise_hbm, res_hbm, dir_hbm, image_out, alpha_out, beta_out,
           pts, scale, noise, res, direc,
           cols, rowpay, rowland, amat, dmat, acc_i, acc_j, back_i, back_j, ks, ks2, ret, stat, stat2, land1, land2,
           in_sem, col_sem, row_sem, pay_sem, fwd_sem, ret_sem, back_sem, s1_sem, s2_sem, st_sem):
    p, q = place()
    turn = 1 - 2 * lax.rem(q, 2)
    barrier = pltpu.get_barrier_semaphore()

    def greet(k, c):
        pl.semaphore_signal(barrier, inc=1, device_id=device(p + k, q), device_id_type=MESH)
        pl.semaphore_signal(barrier, inc=1, device_id=device(p, q + k), device_id_type=MESH)
        return c

    lax.fori_loop(1, SIDE, greet, 0)
    fetch = [pltpu.make_async_copy(a, b, in_sem.at[n]) for n, (a, b) in enumerate(
        ((pts_hbm, pts), (scale_hbm, scale), (dir_hbm, direc), (res_hbm, res), (noise_hbm, noise)))]
    for f in fetch:
        f.start()
    for k in range(SIDE):
        cols[k, PAY:, :] = jnp.zeros((128 - PAY, BLK), BF16)
    acc_i[...] = jnp.zeros_like(acc_i)
    for f in fetch[:3]:
        f.wait()

    at = lax.broadcasted_iota(jnp.int32, (DIM, DIM), 0) == lax.broadcasted_iota(jnp.int32, (DIM, DIM), 1)
    scale_col = jnp.sum(jnp.where(at, scale[...], 0.0), axis=1, keepdims=True)
    scaled = (pts[...] / scale_col).astype(BF16)
    wide = scaled.astype(F32)
    sq = jnp.sum(wide * wide, axis=0, keepdims=True)
    hi = sq.astype(BF16).astype(F32)
    mid = (sq - hi).astype(BF16).astype(F32)
    low = sq - hi - mid
    row = lax.broadcasted_iota(jnp.int32, (AUG, BLK), 0)

    def aug(ones, parts):
        out = jnp.where((row >= ones) & (row < ones + 3), 1.0, 0.0)
        for n, part in enumerate((hi, mid, low)):
            out = jnp.where(row == parts + n, part, out)
        return out.astype(BF16)

    dir_b = direc[...].astype(BF16)
    cols[0, 0:DIM, :] = scaled
    cols[0, DIM:FEAT, :] = aug(0, 3)
    cols[0, FEAT:PAY, :] = dir_b
    rowpay[0:DIM, :] = (wide * -2.0).astype(BF16)
    rowpay[DIM:FEAT, :] = aug(3, 0)
    rowpay[FEAT:PAY, :] = dir_b

    pl.semaphore_wait(barrier, 2 * (SIDE - 1))

    def send_row(k):
        return pltpu.make_async_remote_copy(
            src_ref=rowpay, dst_ref=rowland.at[k], send_sem=pay_sem, recv_sem=row_sem.at[k],
            device_id=device(p - ROWS[k], q), device_id_type=MESH)

    def send_col(k, to=None, sem=None):
        k, to = slot(k), slot(k if to is None else to)
        return pltpu.make_async_remote_copy(
            src_ref=cols.at[k, pl.ds(0, PAY)], dst_ref=cols.at[to, pl.ds(0, PAY)],
            send_sem=pay_sem if sem is None else sem,
            recv_sem=col_sem.at[to], device_id=device(p, q + k - to), device_id_type=MESH)

    def arrived(k):
        send_col(k, k).wait_recv()

    def share_core(k):
        send_col(k, k - turn, fwd_sem).start()

    for k in range(1, 4):
        send_row(k).start()
    send_col(0, 2).start()
    send_col(0, -2).start()
    share_core(0)
    send_col(0, 4).start()
    send_col(0, -4).start()

    def take_row(k, block):
        wide = jnp.concatenate([block[0:FEAT, :], jnp.zeros((128 - FEAT, BLK), BF16)], axis=0)
        amat[k * BLK:(k + 1) * BLK, :] = wide.T
        dmat[:, k * BLK:(k + 1) * BLK] = block[FEAT:PAY, :]

    take_row(0, rowpay)
    for k in range(4, 9):
        send_row(k).start()
    for k in range(1, 4):
        send_row(k).wait_recv()
        take_row(k, rowland.at[k])

    def tile(rows, c):
        a = amat[rows[0] * BLK:rows[1] * BLK, :]
        return matern(jnp.dot(a, cols[slot(c)], preferred_element_type=F32))

    def height(rows):
        return (rows[1] - rows[0]) * BLK

    def give(rows, c, kern, twice=False):
        first = rows[0] + 1 if twice else rows[0]
        skip = (first - rows[0]) * BLK
        k = slot(c)
        part = jnp.dot(dmat[:, first * BLK:rows[1] * BLK], kern[skip:, :], preferred_element_type=F32)
        if rows[1] <= 4:
            acc_j[k] = part
        elif isinstance(c, int) and c == 0:
            acc_j[k] += part
        else:
            back_j[k] = (acc_j[k] + part).astype(BF16)
        part = lax.dot_general(cols[k, FEAT:PAY, :], kern, NT, preferred_element_type=F32)
        for n, r in enumerate(range(*rows)):
            acc_i[r] += part[:, n * BLK:(n + 1) * BLK]

    def step(rows, c, old, c_old, src, dst, twice=False):
        new = tile(rows, c)
        give(old, c_old, src[0:height(old), :], twice)
        dst[0:height(rows), :] = new

    def back_row(k):
        return pltpu.make_async_remote_copy(
            src_ref=back_i.at[k - 1], dst_ref=ret.at[k - 1], send_sem=back_sem, recv_sem=ret_sem,
            device_id=device(p + ROWS[k], q), device_id_type=MESH)

    def back_col(k):
        k = slot(k)
        return pltpu.make_async_remote_copy(
            src_ref=back_j.at[k], dst_ref=ret.at[k + 7], send_sem=back_sem, recv_sem=ret_sem,
            device_id=device(p, q + k), device_id_type=MESH)

    ks[0:height(F1), :] = tile(F1, 0)
    for k in (2, -2):
        arrived(k)
        share_core(k)
    arrived(1)
    arrived(-1)
    step(F1, 1, F1, 0, ks, ks2, twice=True)

    def near(m, carry):
        @pl.when(m == 2)
        def _():
            for k in (4, -4):
                arrived(k)
                share_core(k)
            send_col(4, 6).start()
            send_col(-4, -6).start()
            send_col(4, 8).start()
            arrived(3)
            arrived(-3)

        step(M1, -m, F1, m, ks2, ks)
        step(F1, m + 1, M1, -m, ks, ks2)
        return carry

    lax.fori_loop(1, 4, near, 0)
    step(M1, -4, F1, 4, ks2, ks)

    for k in range(4, 9):
        send_row(k).wait_recv()
        take_row(k, rowland.at[k])
    step(F2, 4, M1, -4, ks, ks2)

    def home_near(n, carry):
        m = 4 - n
        step(M2, -m, F2, m, ks2, ks)
        back_col(m).start()
        step(F2, m - 1, M2, -m, ks, ks2)
        back_col(-m).start()
        return carry

    lax.fori_loop(0, 2, home_near, 0)
    for k in (6, -6, 8):
        arrived(k)
        share_core(k)
    step(M2, -2, F2, 2, ks2, ks)
    back_col(2).start()

    for k in (5, -5, 7, -7):
        arrived(k)
    step(F1, 5, M2, -2, ks, ks2)
    back_col(-2).start()

    def far(m, carry):
        step(M1, -m, F1, m, ks2, ks)
        step(F1, m + 1, M1, -m, ks, ks2)
        return carry

    lax.fori_loop(5, 8, far, 0)

    step(F2, 8, F1, 8, ks2, ks, twice=True)
    for k in range(1, 4):
        back_i[k - 1] = acc_i[k].astype(BF16)
        back_row(k).start()
    step(F2, 7, F2, 8, ks, ks2, twice=True)
    back_col(8).start()

    def home(n, carry):
        m = jnp.where(n < 3, 7 - n, 1)
        step(M2, -m, F2, m, ks2, ks)
        back_col(m).start()
        step(F2, jnp.where(n < 2, 6 - n, 3 - n), M2, -m, ks, ks2)
        back_col(-m).start()
        return carry

    lax.fori_loop(0, 4, home, 0)
    give(F2, 0, ks2[0:height(F2), :], twice=True)
    for k in range(4, 9):
        back_i[k - 1] = acc_i[k].astype(BF16)
        back_row(k).start()

    total = acc_i[0] + acc_j[0]
    for f in fetch[3:]:
        f.wait()
    pltpu.make_async_remote_copy(src_ref=ret, dst_ref=ret, send_sem=back_sem, recv_sem=ret_sem,
                                 device_id=device(p + 1, q), device_id_type=MESH).wait_recv()
    for k in range(23):
        total += ret[k].astype(F32)
    d, r = direc[...], res[...]
    image = total * (5.0 / 3.0) + noise[...] * d
    image_out[...] = image
    lane = lax.broadcasted_iota(jnp.int32, (RHS, 128), 1)
    rhs = lax.broadcasted_iota(jnp.int32, (RHS, 128), 0)

    packed = jnp.zeros((RHS, 128), F32)
    for n, v in enumerate((r * r, d * image, r * image, image * image)):
        packed = jnp.where(lane == rhs + n * RHS, jnp.sum(v, axis=1, keepdims=True), packed)
    stat[...] = jnp.sum(packed, axis=0, keepdims=True)

    def share(src, land, sem, along_p):
        def copy(k):
            to = device(p - k, q) if along_p else device(p, q - k)
            return pltpu.make_async_remote_copy(src_ref=src, dst_ref=land.at[k - 1], send_sem=st_sem,
                                                recv_sem=sem, device_id=to, device_id_type=MESH)

        def start(n, c):
            copy(8 + ((n + 1) // 2) * (1 - 2 * lax.rem(n, 2))).start()
            return c

        lax.fori_loop(0, SIDE - 1, start, 0)
        pltpu.make_async_remote_copy(src_ref=land, dst_ref=land, send_sem=st_sem, recv_sem=sem,
                                     device_id=device(p + 1, q), device_id_type=MESH).wait_recv()
        out = src[...]
        for k in range(SIDE - 1):
            out += land[k]
        return out

    stat2[...] = share(stat, land1, s1_sem, False)
    sums = share(stat2, land2, s2_sem, True)
    rr, curv, rq, qq = (jnp.sum(jnp.where(lane == rhs + n * RHS, sums, 0.0), axis=1, keepdims=True)
                        for n in range(4))
    alpha = rr / curv
    new_rr = rr - alpha * (2.0 * rq - alpha * qq)
    alpha_out[...] = jnp.broadcast_to(alpha, (RHS, BLK))
    beta_out[...] = jnp.broadcast_to(new_rr / rr, (RHS, BLK))

    def sent(ref, sem):
        pltpu.make_async_remote_copy(src_ref=ref, dst_ref=ref, send_sem=sem, recv_sem=ret_sem,
                                     device_id=device(p + 1, q), device_id_type=MESH).wait_send()

    sent(rowland.at[pl.ds(1, 8)], pay_sem)
    for k in range(7):
        sent(rowpay, pay_sem)
    sent(rowland.at[pl.ds(1, 8)], fwd_sem)
    sent(ret, back_sem)
    sent(land1, st_sem)
    sent(land2, st_sem)


def local(points, lengthscale, noise, solution, residual, direction):
    vmem = pl.BlockSpec(memory_space=pltpu.VMEM)
    out = jax.ShapeDtypeStruct((RHS, BLK), F32)
    dma = pltpu.SemaphoreType.DMA
    res_t, dir_t = residual.T, direction.T
    image, alpha, beta = pl.pallas_call(
        kernel,
        out_shape=(out, out, out),
        in_specs=[pl.BlockSpec(memory_space=pltpu.HBM)] * 5,
        out_specs=(vmem,) * 3,
        scratch_shapes=[
            pltpu.VMEM((DIM, BLK), F32),
            pltpu.VMEM((1, DIM), F32),
            pltpu.VMEM((1, BLK), F32),
            pltpu.VMEM((RHS, BLK), F32),
            pltpu.VMEM((RHS, BLK), F32),
            pltpu.VMEM((SIDE, 128, BLK), BF16),
            pltpu.VMEM((PAY, BLK), BF16),
            pltpu.VMEM((9, PAY, BLK), BF16),
            pltpu.VMEM((9 * BLK, 128), BF16),
            pltpu.VMEM((RHS, 9 * BLK), BF16),
            pltpu.VMEM((9, RHS, BLK), F32),
            pltpu.VMEM((SIDE, RHS, BLK), F32),
            pltpu.VMEM((8, RHS, BLK), BF16),
            pltpu.VMEM((SIDE, RHS, BLK), BF16),
            pltpu.VMEM((5 * BLK, BLK), BF16),
            pltpu.VMEM((5 * BLK, BLK), BF16),
            pltpu.VMEM((23, RHS, BLK), BF16),
            pltpu.VMEM((1, 128), F32),
            pltpu.VMEM((1, 128), F32),
            pltpu.VMEM((SIDE - 1, 1, 128), F32),
            pltpu.VMEM((SIDE - 1, 1, 128), F32),
            dma((5,)),
            dma((SIDE,)),
            dma((9,)),
        ] + [dma] * 7,
        compiler_params=pltpu.CompilerParams(
            collective_id=0, has_side_effects=True, vmem_limit_bytes=63 * 2**20),
        name="cg_step",
    )(points.T, lengthscale[None, :], noise[None, :], res_t, dir_t)
    new_sol = solution.T + alpha * dir_t
    new_res = res_t - alpha * image
    new_dir = new_res + beta * dir_t
    return new_sol.T, new_res.T, new_dir.T


def solution(mesh):
    rows = P(("blk", "grp"), None)
    in_specs = (rows, P(), P(("blk", "grp")), rows, rows, rows)
    return jax.shard_map(local, mesh=mesh, in_specs=in_specs, out_specs=(rows,) * 3, check_vma=False)
```

time: 66.9 us -> 53.1 us (0.79); the launches traced: 65.9 us -> 52.9 us
  Pallas kernels: 60.2 us -> 50.8 us
  local copies, waits for them, and re-layouts: 4.96 us -> 0.01 us
  other arithmetic: 0 us -> 1.44 us
    pallas_call x1, Pallas kernels: 60.2 us -> 50.8 us  [local(): pl.pallas_call(kernel, out_shape=(out, out, out), in_specs=[pl.BlockSpec(...]
    unnamed x13 -> x6, local copies, waits for them, and re-layouts: 4.2 us -> 0.01 us
    transpose x0 -> x1, other arithmetic: none -> 1.44 us  [local(): return (new_sol.T, new_res.T, new_dir.T)]
    broadcast_in_dim x1 -> x0, local copies, waits for them, and re-layouts: 0.76 us -> none  [local(): lengthscale[:, None]]
where the time goes in v2:
time: 53.1 us; the launch traced here: 52.9 us
  Pallas kernels  50.8 us (96%)
  other arithmetic  1.44 us (3%)
  between operations  0.69 us (1%)
    pallas_call x1, Pallas kernels, local(): pl.pallas_call(kernel, out_shape=(out, out, out), in_specs=[pl.BlockSpec(...  50.8 us
    transpose x1, other arithmetic, local(): return (new_sol.T, new_res.T, new_dir.T)  1.44 us

profile of v2, /device:TPU:1, one launch (start us, length us, event | category | flops | bytes accessed | tf_op | source)
XLA Modules:
  0.0 52.9 jit_solution(14022569747698127655)
XLA Ops:
  0.6 0.0 copy-start
  0.6 0.0 copy-start.1
  0.7 0.0 copy-start.2
  0.7 50.8 %cg_step.1 = (f32[32,256]{1,0:T(8,128)}, f32[32,256]{1,0:T(8,128)}, f32[32,256]{1,0:T(8,128)}) custom-call(f32[64,256]{1,0:T(8,128)} %bitcast.24, f32[1,64]{1,0:T(1,128)} %bitcast.26, f32[1,256]{1,0:T(1,128)} %bitcast.25, f32[32,256]{1,0:T(8,128)} %bitcast.22, f32[32,256]{1,0:T(8,128)} %bitcast.23), custom_call_target="tpu_custom_call" | custom-call | tf_op jit(solution)/shard_map/cg_step/pallas_call | solution.py:319
  51.5 0.0 copy-done
  51.5 0.0 copy-done.1
  51.5 0.0 copy-done.2
  51.5 1.4 %add_bitcast_fusion = (f32[256,32]{0,1:T(8,128)}, f32[256,32]{0,1:T(8,128)}, f32[256,32]{0,1:T(8,128)}) fusion(f32[32,256]{1,0:T(8,128)} %get-tuple-element.8, f32[256,32]{0,1:T(8,128)S(1)} %copy-done.1, f32[32,256]{1,0:T(8,128)} %get-tuple-element.6, f32[32,256]{1,0:T(8,128)} %get-tuple-element.7, f32[256,32]{0,1:T(8,128)S(1)} %copy-done, ...), kind=kLoop, calls=%fused_computation.2 | loop fusion | flops 49152 | bytes 294912 | tf_op jit(solution)/shard_map/transpose | solution.py:357
Async XLA Ops:
  0.6 50.8 %copy-start = (f32[256,32]{0,1:T(8,128)S(1)}, f32[256,32]{0,1:T(8,128)}, u32[]{:S(2)}) copy-start(f32[256,32]{0,1:T(8,128)} %param.10) | copy-start | bytes 98308
  0.6 50.8 %copy-start.1 = (f32[256,32]{0,1:T(8,128)S(1)}, f32[256,32]{0,1:T(8,128)}, u32[]{:S(2)}) copy-start(f32[256,32]{0,1:T(8,128)} %param.11) | copy-start | bytes 98308
  0.7 50.8 %copy-start.2 = (f32[256,32]{0,1:T(8,128)S(1)}, f32[256,32]{0,1:T(8,128)}, u32[]{:S(2)}) copy-start(f32[256,32]{0,1:T(8,128)} %param.9) | copy-start | bytes 98308

commit v3 on v2

--- a/solution.py
+++ b/solution.py
@@ -17,11 +17,10 @@
 FEAT = DIM + AUG
 PAY = FEAT + RHS
 SIDE = 16
-PANEL1 = (0, 1, -4, 3)
-PANEL2 = (8, -5, 2, 6, -7)
-ROWS = PANEL1 + PANEL2
-F1, M1 = (0, 4), (1, 4)
-F2, M2 = (4, 9), (5, 9)
+NEAR = (-1, 4, -3, 5)
+FAR = (8, -2, 6, -7)
+ROWS = (0,) + NEAR + FAR
+F1, F2, M2 = (1, 5), (5, 9), (6, 9)
 EXPO = -3.2259641843312467
 LIN = 1.3416407864998738
 
@@ -115,13 +114,11 @@
     def share_core(k):
         send_col(k, k - turn, fwd_sem).start()
 
-    for k in range(1, 4):
+    for k in range(*F1):
         send_row(k).start()
     send_col(0, 2).start()
     send_col(0, -2).start()
     share_core(0)
-    send_col(0, 4).start()
-    send_col(0, -4).start()
 
     def take_row(k, block):
         wide = jnp.concatenate([block[0:FEAT, :], jnp.zeros((128 - FEAT, BLK), BF16)], axis=0)
@@ -129,11 +126,16 @@
         dmat[:, k * BLK:(k + 1) * BLK] = block[FEAT:PAY, :]
 
     take_row(0, rowpay)
-    for k in range(4, 9):
-        send_row(k).start()
-    for k in range(1, 4):
+    for k in (2, -2):
+        arrived(k)
+        share_core(k)
+    send_col(0, 4).start()
+    send_col(0, -4).start()
+    for k in range(*F1):
         send_row(k).wait_recv()
         take_row(k, rowland.at[k])
+    for k in range(*F2):
+        send_row(k).start()
 
     def tile(rows, c):
         a = amat[rows[0] * BLK:rows[1] * BLK, :]
@@ -147,7 +149,7 @@
         skip = (first - rows[0]) * BLK
         k = slot(c)
         part = jnp.dot(dmat[:, first * BLK:rows[1] * BLK], kern[skip:, :], preferred_element_type=F32)
-        if rows[1] <= 4:
+        if rows == F1:
             acc_j[k] = part
         elif isinstance(c, int) and c == 0:
             acc_j[k] += part
@@ -173,16 +175,26 @@
             src_ref=back_j.at[k], dst_ref=ret.at[k + 7], send_sem=back_sem, recv_sem=ret_sem,
             device_id=device(p, q + k), device_id_type=MESH)
 
-    ks[0:height(F1), :] = tile(F1, 0)
-    for k in (2, -2):
-        arrived(k)
-        share_core(k)
+    def own_tile(n):
+        a = amat[0:BLK, :]
+        return [matern(jnp.dot(a, cols[4 * n + i], preferred_element_type=F32)) for i in range(4)]
+
+    def own_give(n, src):
+        acc_i[0] += sum(lax.dot_general(cols[4 * n + i, FEAT:PAY, :], src[i * BLK:(i + 1) * BLK, :], NT,
+                                        preferred_element_type=F32) for i in range(4))
+
+    def own_put(new, dst):
+        for i, kern in enumerate(new):
+            dst[i * BLK:(i + 1) * BLK, :] = kern
+
+    ks[...] = tile(F1, 0)
     arrived(1)
     arrived(-1)
-    step(F1, 1, F1, 0, ks, ks2, twice=True)
-
-    def near(m, carry):
-        @pl.when(m == 2)
+
+    def near(n, last):
+        k = jnp.where(n < 3, n, 7 - n)
+
+        @pl.when(n == 3)
         def _():
             for k in (4, -4):
                 arrived(k)
@@ -190,20 +202,22 @@
             send_col(4, 6).start()
             send_col(-4, -6).start()
             send_col(4, 8).start()
+
+        @pl.when(n == 4)
+        def _():
             arrived(3)
             arrived(-3)
 
-        step(M1, -m, F1, m, ks2, ks)
-        step(F1, m + 1, M1, -m, ks, ks2)
-        return carry
-
-    lax.fori_loop(1, 4, near, 0)
-    step(M1, -4, F1, 4, ks2, ks)
-
-    for k in range(4, 9):
+        step(F1, k, F1, last, ks, ks2)
+        step(F1, -k, F1, k, ks2, ks)
+        return -k
+
+    lax.fori_loop(1, 5, near, jnp.int32(0))
+
+    for k in range(*F2):
         send_row(k).wait_recv()
         take_row(k, rowland.at[k])
-    step(F2, 4, M1, -4, ks, ks2)
+    step(F2, 4, F1, -3, ks, ks2)
 
     def home_near(n, carry):
         m = 4 - n
@@ -226,14 +240,14 @@
     back_col(-2).start()
 
     def far(m, carry):
-        step(M1, -m, F1, m, ks2, ks)
-        step(F1, m + 1, M1, -m, ks, ks2)
+        step(F1, -m, F1, m, ks2, ks)
+        step(F1, m + 1, F1, -m, ks, ks2)
         return carry
 
     lax.fori_loop(5, 8, far, 0)
 
-    step(F2, 8, F1, 8, ks2, ks, twice=True)
-    for k in range(1, 4):
+    step(F2, 8, F1, 8, ks2, ks)
+    for k in range(*F1):
         back_i[k - 1] = acc_i[k].astype(BF16)
         back_row(k).start()
     step(F2, 7, F2, 8, ks, ks2, twice=True)
@@ -248,10 +262,19 @@
         return carry
 
     lax.fori_loop(0, 4, home, 0)
-    give(F2, 0, ks2[0:height(F2), :], twice=True)
-    for k in range(4, 9):
+    new = own_tile(0)
+    give(F2, 0, ks2[...], twice=True)
+    own_put(new, ks)
+    for k in range(*F2):
         back_i[k - 1] = acc_i[k].astype(BF16)
         back_row(k).start()
+
+    for n in range(1, 4):
+        src, dst = (ks, ks2) if n % 2 else (ks2, ks)
+        new = own_tile(n)
+        own_give(n - 1, src)
+        own_put(new, dst)
+    own_give(3, ks2)
 
     total = acc_i[0] + acc_j[0]
     for f in fetch[3:]:
@@ -277,11 +300,11 @@
             return pltpu.make_async_remote_copy(src_ref=src, dst_ref=land.at[k - 1], send_sem=st_sem,
                                                 recv_sem=sem, device_id=to, device_id_type=MESH)
 
-        def start(n, c):
-            copy(8 + ((n + 1) // 2) * (1 - 2 * lax.rem(n, 2))).start()
+        def start(k, c):
+            copy(k).start()
             return c
 
-        lax.fori_loop(0, SIDE - 1, start, 0)
+        lax.fori_loop(1, SIDE, start, 0)
         pltpu.make_async_remote_copy(src_ref=land, dst_ref=land, send_sem=st_sem, recv_sem=sem,
                                      device_id=device(p + 1, q), device_id_type=MESH).wait_recv()
         out = src[...]
@@ -336,8 +359,8 @@
             pltpu.VMEM((SIDE, RHS, BLK), F32),
             pltpu.VMEM((8, RHS, BLK), BF16),
             pltpu.VMEM((SIDE, RHS, BLK), BF16),
-            pltpu.VMEM((5 * BLK, BLK), BF16),
-            pltpu.VMEM((5 * BLK, BLK), BF16),
+            pltpu.VMEM((4 * BLK, BLK), BF16),
+            pltpu.VMEM((4 * BLK, BLK), BF16),
             pltpu.VMEM((23, RHS, BLK), BF16),
             pltpu.VMEM((1, 128), F32),
             pltpu.VMEM((1, 128), F32),

time: 53.1 us -> 50.9 us (0.959)
  Pallas kernels: 50.8 us -> 48.5 us
    pallas_call x1, Pallas kernels: 50.8 us -> 48.5 us  [local(): pl.pallas_call(kernel, out_shape=(out, out, out), in_specs=[pl.BlockSpec(...]
where the time goes in v3:
time: 50.9 us; the launch traced here: 50.7 us
  Pallas kernels  48.5 us (95%)
  other arithmetic  1.44 us (3%)
  between operations  0.69 us (1%)
    pallas_call x1, Pallas kernels, local(): pl.pallas_call(kernel, out_shape=(out, out, out), in_specs=[pl.BlockSpec(...  48.5 us
    transpose x1, other arithmetic, local(): return (new_sol.T, new_res.T, new_dir.T)  1.44 us

profile of v3, /device:TPU:1, one launch (start us, length us, event | category | flops | bytes accessed | tf_op | source)
XLA Modules:
  0.0 50.7 jit_solution(9922897382016318965)
XLA Ops:
  0.6 0.0 copy-start
  0.6 0.0 copy-start.1
  0.7 0.0 copy-start.2
  0.7 48.5 %cg_step.1 = (f32[32,256]{1,0:T(8,128)}, f32[32,256]{1,0:T(8,128)}, f32[32,256]{1,0:T(8,128)}) custom-call(f32[64,256]{1,0:T(8,128)} %bitcast.24, f32[1,64]{1,0:T(1,128)} %bitcast.26, f32[1,256]{1,0:T(1,128)} %bitcast.25, f32[32,256]{1,0:T(8,128)} %bitcast.22, f32[32,256]{1,0:T(8,128)} %bitcast.23), custom_call_target="tpu_custom_call" | custom-call | tf_op jit(solution)/shard_map/cg_step/pallas_call | solution.py:342
  49.2 0.0 copy-done
  49.2 0.0 copy-done.1
  49.2 0.0 copy-done.2
  49.2 1.4 %add_bitcast_fusion = (f32[256,32]{0,1:T(8,128)}, f32[256,32]{0,1:T(8,128)}, f32[256,32]{0,1:T(8,128)}) fusion(f32[32,256]{1,0:T(8,128)} %get-tuple-element.8, f32[256,32]{0,1:T(8,128)S(1)} %copy-done.1, f32[32,256]{1,0:T(8,128)} %get-tuple-element.6, f32[32,256]{1,0:T(8,128)} %get-tuple-element.7, f32[256,32]{0,1:T(8,128)S(1)} %copy-done, ...), kind=kLoop, calls=%fused_computation.2 | loop fusion | flops 49152 | bytes 294912 | tf_op jit(solution)/shard_map/transpose | solution.py:380
Async XLA Ops:
  0.6 48.6 %copy-start = (f32[256,32]{0,1:T(8,128)S(1)}, f32[256,32]{0,1:T(8,128)}, u32[]{:S(2)}) copy-start(f32[256,32]{0,1:T(8,128)} %param.10) | copy-start | bytes 98308
  0.6 48.6 %copy-start.1 = (f32[256,32]{0,1:T(8,128)S(1)}, f32[256,32]{0,1:T(8,128)}, u32[]{:S(2)}) copy-start(f32[256,32]{0,1:T(8,128)} %param.11) | copy-start | bytes 98308
  0.7 48.6 %copy-start.2 = (f32[256,32]{0,1:T(8,128)S(1)}, f32[256,32]{0,1:T(8,128)}, u32[]{:S(2)}) copy-start(f32[256,32]{0,1:T(8,128)} %param.9) | copy-start | bytes 98308

commit v4 on v3

--- a/solution.py
+++ b/solution.py
@@ -20,7 +20,9 @@
 NEAR = (-1, 4, -3, 5)
 FAR = (8, -2, 6, -7)
 ROWS = (0,) + NEAR + FAR
+A1, B1 = (1, 3), (3, 5)
 F1, F2, M2 = (1, 5), (5, 9), (6, 9)
+FAR_FIRST = (8, 7, 9, 6, 10, 5, 11, 4, 12, 3, 13, 2, 14, 1, 15)
 EXPO = -3.2259641843312467
 LIN = 1.3416407864998738
 
@@ -33,13 +35,14 @@
 
 def place():
     g, b = lax.axis_index("grp"), lax.axis_index("blk")
-    return (b // 4) * 4 + (g // 8) * 2 + (b // 2) % 2, (g % 8) * 2 + b % 2
+    return (lax.div(b, 4) * 4 + lax.div(g, 8) * 2 + lax.rem(lax.div(b, 2), 2),
+            lax.rem(g, 8) * 2 + lax.rem(b, 2))
 
 
 def device(p, q):
     p, q = lax.rem(p + 32, SIDE), lax.rem(q + 32, SIDE)
-    x, y = p // 4, p % 4
-    return {"grp": (y // 2) * 8 + q // 2, "blk": x * 4 + (y % 2) * 2 + q % 2}
+    x, y = lax.div(p, 4), lax.rem(p, 4)
+    return {"grp": lax.div(y, 2) * 8 + lax.div(q, 2), "blk": x * 4 + lax.rem(y, 2) * 2 + lax.rem(q, 2)}
 
 
 def slot(k):
@@ -54,12 +57,9 @@
     turn = 1 - 2 * lax.rem(q, 2)
     barrier = pltpu.get_barrier_semaphore()
 
-    def greet(k, c):
+    for k in FAR_FIRST:
         pl.semaphore_signal(barrier, inc=1, device_id=device(p + k, q), device_id_type=MESH)
         pl.semaphore_signal(barrier, inc=1, device_id=device(p, q + k), device_id_type=MESH)
-        return c
-
-    lax.fori_loop(1, SIDE, greet, 0)
     fetch = [pltpu.make_async_copy(a, b, in_sem.at[n]) for n, (a, b) in enumerate(
         ((pts_hbm, pts), (scale_hbm, scale), (dir_hbm, direc), (res_hbm, res), (noise_hbm, noise)))]
     for f in fetch:
@@ -119,6 +119,10 @@
     send_col(0, 2).start()
     send_col(0, -2).start()
     share_core(0)
+    send_col(0, 4).start()
+    send_col(0, -4).start()
+    for k in range(*F2):
+        send_row(k).start()
 
     def take_row(k, block):
         wide = jnp.concatenate([block[0:FEAT, :], jnp.zeros((128 - FEAT, BLK), BF16)], axis=0)
@@ -129,13 +133,9 @@
     for k in (2, -2):
         arrived(k)
         share_core(k)
-    send_col(0, 4).start()
-    send_col(0, -4).start()
-    for k in range(*F1):
+    for k in range(*A1):
         send_row(k).wait_recv()
         take_row(k, rowland.at[k])
-    for k in range(*F2):
-        send_row(k).start()
 
     def tile(rows, c):
         a = amat[rows[0] * BLK:rows[1] * BLK, :]
@@ -149,8 +149,10 @@
         skip = (first - rows[0]) * BLK
         k = slot(c)
         part = jnp.dot(dmat[:, first * BLK:rows[1] * BLK], kern[skip:, :], preferred_element_type=F32)
-        if rows == F1:
+        if rows in (A1, F1):
             acc_j[k] = part
+        elif rows == B1:
+            acc_j[k] += part
         elif isinstance(c, int) and c == 0:
             acc_j[k] += part
         else:
@@ -187,32 +189,33 @@
         for i, kern in enumerate(new):
             dst[i * BLK:(i + 1) * BLK, :] = kern
 
-    ks[...] = tile(F1, 0)
+    ks2[0:height(A1), :] = tile(A1, 0)
+    step(A1, 2, A1, 0, ks2, ks)
+    step(A1, -2, A1, 2, ks, ks2)
     arrived(1)
     arrived(-1)
-
-    def near(n, last):
-        k = jnp.where(n < 3, n, 7 - n)
-
-        @pl.when(n == 3)
-        def _():
-            for k in (4, -4):
-                arrived(k)
-                share_core(k)
-            send_col(4, 6).start()
-            send_col(-4, -6).start()
-            send_col(4, 8).start()
-
-        @pl.when(n == 4)
-        def _():
-            arrived(3)
-            arrived(-3)
-
-        step(F1, k, F1, last, ks, ks2)
-        step(F1, -k, F1, k, ks2, ks)
-        return -k
-
-    lax.fori_loop(1, 5, near, jnp.int32(0))
+    step(A1, 1, A1, -2, ks2, ks)
+    step(A1, -1, A1, 1, ks, ks2)
+    for k in (4, -4):
+        arrived(k)
+        share_core(k)
+    send_col(4, 6).start()
+    send_col(-4, -6).start()
+    send_col(4, 8).start()
+    for k in range(*B1):
+        send_row(k).wait_recv()
+        take_row(k, rowland.at[k])
+    step(B1, 0, A1, -1, ks2, ks)
+    step(B1, 2, B1, 0, ks, ks2)
+    step(B1, -2, B1, 2, ks2, ks)
+    step(B1, 1, B1, -2, ks, ks2)
+    step(B1, -1, B1, 1, ks2, ks)
+    step(F1, 4, B1, -1, ks, ks2)
+    step(F1, -4, F1, 4, ks2, ks)
+    arrived(3)
+    arrived(-3)
+    step(F1, 3, F1, -4, ks, ks2)
+    step(F1, -3, F1, 3, ks2, ks)
 
     for k in range(*F2):
         send_row(k).wait_recv()
@@ -300,11 +303,8 @@
             return pltpu.make_async_remote_copy(src_ref=src, dst_ref=land.at[k - 1], send_sem=st_sem,
                                                 recv_sem=sem, device_id=to, device_id_type=MESH)
 
-        def start(k, c):
+        for k in FAR_FIRST:
             copy(k).start()
-            return c
-
-        lax.fori_loop(1, SIDE, start, 0)
         pltpu.make_async_remote_copy(src_ref=land, dst_ref=land, send_sem=st_sem, recv_sem=sem,
                                      device_id=device(p + 1, q), device_id_type=MESH).wait_recv()
         out = src[...]

time: 50.9 us -> 48.6 us (0.955)
  Pallas kernels: 48.5 us -> 46.3 us
    pallas_call x1, Pallas kernels: 48.5 us -> 46.3 us  [local(): pl.pallas_call(kernel, out_shape=(out, out, out), in_specs=[pl.BlockSpec(...]
where the time goes in v4:
time: 48.6 us; the launch traced here: 48.4 us
  Pallas kernels  46.3 us (95%)
  other arithmetic  1.44 us (3%)
  between operations  0.69 us (1%)
    pallas_call x1, Pallas kernels, local(): pl.pallas_call(kernel, out_shape=(out, out, out), in_specs=[pl.BlockSpec(...  46.3 us
    transpose x1, other arithmetic, local(): return (new_sol.T, new_res.T, new_dir.T)  1.44 us

profile of v4, /device:TPU:1, one launch (start us, length us, event | category | flops | bytes accessed | tf_op | source)
XLA Modules:
  0.0 48.4 jit_solution(6095196324652424856)
XLA Ops:
  0.6 0.0 copy-start
  0.6 0.0 copy-start.1
  0.7 0.0 copy-start.2
  0.7 46.3 %cg_step.1 = (f32[32,256]{1,0:T(8,128)}, f32[32,256]{1,0:T(8,128)}, f32[32,256]{1,0:T(8,128)}) custom-call(f32[64,256]{1,0:T(8,128)} %bitcast.24, f32[1,64]{1,0:T(1,128)} %bitcast.26, f32[1,256]{1,0:T(1,128)} %bitcast.25, f32[32,256]{1,0:T(8,128)} %bitcast.22, f32[32,256]{1,0:T(8,128)} %bitcast.23), custom_call_target="tpu_custom_call" | custom-call | tf_op jit(solution)/shard_map/cg_step/pallas_call | solution.py:342
  46.9 0.0 copy-done
  46.9 0.0 copy-done.1
  47.0 0.0 copy-done.2
  47.0 1.4 %add_bitcast_fusion = (f32[256,32]{0,1:T(8,128)}, f32[256,32]{0,1:T(8,128)}, f32[256,32]{0,1:T(8,128)}) fusion(f32[32,256]{1,0:T(8,128)} %get-tuple-element.8, f32[256,32]{0,1:T(8,128)S(1)} %copy-done.1, f32[32,256]{1,0:T(8,128)} %get-tuple-element.6, f32[32,256]{1,0:T(8,128)} %get-tuple-element.7, f32[256,32]{0,1:T(8,128)S(1)} %copy-done, ...), kind=kLoop, calls=%fused_computation.2 | loop fusion | flops 49152 | bytes 294912 | tf_op jit(solution)/shard_map/transpose | solution.py:380
Async XLA Ops:
  0.6 46.3 %copy-start = (f32[256,32]{0,1:T(8,128)S(1)}, f32[256,32]{0,1:T(8,128)}, u32[]{:S(2)}) copy-start(f32[256,32]{0,1:T(8,128)} %param.10) | copy-start | bytes 98308
  0.6 46.3 %copy-start.1 = (f32[256,32]{0,1:T(8,128)S(1)}, f32[256,32]{0,1:T(8,128)}, u32[]{:S(2)}) copy-start(f32[256,32]{0,1:T(8,128)} %param.11) | copy-start | bytes 98308
  0.7 46.3 %copy-start.2 = (f32[256,32]{0,1:T(8,128)S(1)}, f32[256,32]{0,1:T(8,128)}, u32[]{:S(2)}) copy-start(f32[256,32]{0,1:T(8,128)} %param.9) | copy-start | bytes 98308

commit v5 on v4

--- a/solution.py
+++ b/solution.py
@@ -55,18 +55,17 @@
            in_sem, col_sem, row_sem, pay_sem, fwd_sem, ret_sem, back_sem, s1_sem, s2_sem, st_sem):
     p, q = place()
     turn = 1 - 2 * lax.rem(q, 2)
-    barrier = pltpu.get_barrier_semaphore()
-
-    for k in FAR_FIRST:
-        pl.semaphore_signal(barrier, inc=1, device_id=device(p + k, q), device_id_type=MESH)
-        pl.semaphore_signal(barrier, inc=1, device_id=device(p, q + k), device_id_type=MESH)
     fetch = [pltpu.make_async_copy(a, b, in_sem.at[n]) for n, (a, b) in enumerate(
         ((pts_hbm, pts), (scale_hbm, scale), (dir_hbm, direc), (res_hbm, res), (noise_hbm, noise)))]
     for f in fetch:
         f.start()
+    barrier = pltpu.get_barrier_semaphore()
+
+    for k in FAR_FIRST:
+        pl.semaphore_signal(barrier, inc=1, device_id=device(p + k, q), device_id_type=MESH)
+        pl.semaphore_signal(barrier, inc=1, device_id=device(p, q + k), device_id_type=MESH)
     for k in range(SIDE):
         cols[k, PAY:, :] = jnp.zeros((128 - PAY, BLK), BF16)
-    acc_i[...] = jnp.zeros_like(acc_i)
     for f in fetch[:3]:
         f.wait()
 
@@ -129,6 +128,7 @@
         amat[k * BLK:(k + 1) * BLK, :] = wide.T
         dmat[:, k * BLK:(k + 1) * BLK] = block[FEAT:PAY, :]
 
+    acc_i[...] = jnp.zeros_like(acc_i)
     take_row(0, rowpay)
     for k in (2, -2):
         arrived(k)
@@ -144,17 +144,18 @@
     def height(rows):
         return (rows[1] - rows[0]) * BLK
 
+    far_cols = [False]
+
     def give(rows, c, kern, twice=False):
         first = rows[0] + 1 if twice else rows[0]
         skip = (first - rows[0]) * BLK
         k = slot(c)
         part = jnp.dot(dmat[:, first * BLK:rows[1] * BLK], kern[skip:, :], preferred_element_type=F32)
-        if rows in (A1, F1):
+        near_rows = rows[1] <= F1[1]
+        if rows == B1 or (isinstance(c, int) and c == 0 and not near_rows):
+            acc_j[k] += part
+        elif near_rows != far_cols[0]:
             acc_j[k] = part
-        elif rows == B1:
-            acc_j[k] += part
-        elif isinstance(c, int) and c == 0:
-            acc_j[k] += part
         else:
             back_j[k] = (acc_j[k] + part).astype(BF16)
         part = lax.dot_general(cols[k, FEAT:PAY, :], kern, NT, preferred_element_type=F32)
@@ -198,10 +199,11 @@
     step(A1, -1, A1, 1, ks, ks2)
     for k in (4, -4):
         arrived(k)
-        share_core(k)
     send_col(4, 6).start()
     send_col(-4, -6).start()
     send_col(4, 8).start()
+    for k in (4, -4):
+        share_core(k)
     for k in range(*B1):
         send_row(k).wait_recv()
         take_row(k, rowland.at[k])
@@ -224,51 +226,59 @@
 
     def home_near(n, carry):
         m = 4 - n
+
+        @pl.when(n == 2)
+        def _():
+            for k in (6, -6, 8):
+                arrived(k)
+                share_core(k)
+
         step(M2, -m, F2, m, ks2, ks)
         back_col(m).start()
         step(F2, m - 1, M2, -m, ks, ks2)
         back_col(-m).start()
         return carry
 
-    lax.fori_loop(0, 2, home_near, 0)
-    for k in (6, -6, 8):
-        arrived(k)
-        share_core(k)
-    step(M2, -2, F2, 2, ks2, ks)
-    back_col(2).start()
+    lax.fori_loop(0, 4, home_near, 0)
 
     for k in (5, -5, 7, -7):
         arrived(k)
-    step(F1, 5, M2, -2, ks, ks2)
-    back_col(-2).start()
-
-    def far(m, carry):
-        step(F1, -m, F1, m, ks2, ks)
-        step(F1, m + 1, F1, -m, ks, ks2)
+    step(F2, 8, F2, 0, ks2, ks, twice=True)
+    far_cols[0] = True
+    step(F2, 7, F2, 8, ks, ks2, twice=True)
+
+    def far(n, carry):
+        m = 7 - n
+        step(M2, -m, F2, m, ks2, ks)
+        step(F2, m - 1, M2, -m, ks, ks2)
         return carry
 
-    lax.fori_loop(5, 8, far, 0)
-
-    step(F2, 8, F1, 8, ks2, ks)
-    for k in range(*F1):
+    lax.fori_loop(0, 2, far, 0)
+    step(M2, -5, F2, 5, ks2, ks)
+
+    step(F1, 8, M2, -5, ks, ks2)
+    for k in range(*F2):
         back_i[k - 1] = acc_i[k].astype(BF16)
         back_row(k).start()
-    step(F2, 7, F2, 8, ks, ks2, twice=True)
+    step(F1, 7, F1, 8, ks2, ks)
     back_col(8).start()
 
     def home(n, carry):
-        m = jnp.where(n < 3, 7 - n, 1)
-        step(M2, -m, F2, m, ks2, ks)
+        m = 7 - n
+        step(F1, -m, F1, m, ks, ks2)
         back_col(m).start()
-        step(F2, jnp.where(n < 2, 6 - n, 3 - n), M2, -m, ks, ks2)
+        step(F1, m - 1, F1, -m, ks2, ks)
         back_col(-m).start()
         return carry
 
-    lax.fori_loop(0, 4, home, 0)
+    lax.fori_loop(0, 2, home, 0)
+    step(F1, -5, F1, 5, ks, ks2)
+    back_col(5).start()
     new = own_tile(0)
-    give(F2, 0, ks2[...], twice=True)
+    give(F1, -5, ks2[...])
+    back_col(-5).start()
     own_put(new, ks)
-    for k in range(*F2):
+    for k in range(*F1):
         back_i[k - 1] = acc_i[k].astype(BF16)
         back_row(k).start()
 
@@ -282,20 +292,27 @@
     total = acc_i[0] + acc_j[0]
     for f in fetch[3:]:
         f.wait()
+    d, r = direc[...], res[...]
+    total = total * (5.0 / 3.0) + noise[...] * d
+    rr = jnp.sum(r * r, axis=1, keepdims=True)
     pltpu.make_async_remote_copy(src_ref=ret, dst_ref=ret, send_sem=back_sem, recv_sem=ret_sem,
                                  device_id=device(p + 1, q), device_id_type=MESH).wait_recv()
-    for k in range(23):
-        total += ret[k].astype(F32)
-    d, r = direc[...], res[...]
-    image = total * (5.0 / 3.0) + noise[...] * d
+    parts = [ret[k].astype(F32) for k in range(23)]
+    while len(parts) > 1:
+        parts = [sum(parts[n:n + 2]) for n in range(0, len(parts), 2)]
+    image = total + parts[0] * (5.0 / 3.0)
     image_out[...] = image
     lane = lax.broadcasted_iota(jnp.int32, (RHS, 128), 1)
     rhs = lax.broadcasted_iota(jnp.int32, (RHS, 128), 0)
 
     packed = jnp.zeros((RHS, 128), F32)
-    for n, v in enumerate((r * r, d * image, r * image, image * image)):
-        packed = jnp.where(lane == rhs + n * RHS, jnp.sum(v, axis=1, keepdims=True), packed)
+    for n, v in enumerate((rr, *(jnp.sum(v * image, axis=1, keepdims=True) for v in (d, r, image)))):
+        packed = jnp.where(lane == rhs + n * RHS, v, packed)
     stat[...] = jnp.sum(packed, axis=0, keepdims=True)
+
+    def sent(ref, sem):
+        pltpu.make_async_remote_copy(src_ref=ref, dst_ref=ref, send_sem=sem, recv_sem=ret_sem,
+                                     device_id=device(p + 1, q), device_id_type=MESH).wait_send()
 
     def share(src, land, sem, along_p):
         def copy(k):
@@ -305,6 +322,12 @@
 
         for k in FAR_FIRST:
             copy(k).start()
+        if not along_p:
+            sent(rowland.at[pl.ds(1, 8)], pay_sem)
+            for k in range(7):
+                sent(rowpay, pay_sem)
+            sent(rowland.at[pl.ds(1, 8)], fwd_sem)
+            sent(ret, back_sem)
         pltpu.make_async_remote_copy(src_ref=land, dst_ref=land, send_sem=st_sem, recv_sem=sem,
                                      device_id=device(p + 1, q), device_id_type=MESH).wait_recv()
         out = src[...]
@@ -321,15 +344,6 @@
     alpha_out[...] = jnp.broadcast_to(alpha, (RHS, BLK))
     beta_out[...] = jnp.broadcast_to(new_rr / rr, (RHS, BLK))
 
-    def sent(ref, sem):
-        pltpu.make_async_remote_copy(src_ref=ref, dst_ref=ref, send_sem=sem, recv_sem=ret_sem,
-                                     device_id=device(p + 1, q), device_id_type=MESH).wait_send()
-
-    sent(rowland.at[pl.ds(1, 8)], pay_sem)
-    for k in range(7):
-        sent(rowpay, pay_sem)
-    sent(rowland.at[pl.ds(1, 8)], fwd_sem)
-    sent(ret, back_sem)
     sent(land1, st_sem)
     sent(land2, st_sem)
 

time: 48.6 us -> 47.7 us (0.981)
  Pallas kernels: 46.3 us -> 45.4 us
    pallas_call x1, Pallas kernels: 46.3 us -> 45.4 us  [local(): pl.pallas_call(kernel, out_shape=(out, out, out), in_specs=[pl.BlockSpec(...]
where the time goes in v5:
time: 47.7 us; the launch traced here: 47.5 us
  Pallas kernels  45.4 us (95%)
  other arithmetic  1.44 us (3%)
  between operations  0.69 us (1%)
    pallas_call x1, Pallas kernels, local(): pl.pallas_call(kernel, out_shape=(out, out, out), in_specs=[pl.BlockSpec(...  45.4 us
    transpose x1, other arithmetic, local(): return (new_sol.T, new_res.T, new_dir.T)  1.44 us

profile of v5, /device:TPU:1, one launch (start us, length us, event | category | flops | bytes accessed | tf_op | source)
XLA Modules:
  0.0 47.5 jit_solution(9937676373265684838)
XLA Ops:
  0.6 0.0 copy-start
  0.6 0.0 copy-start.1
  0.7 0.0 copy-start.2
  0.7 45.4 %cg_step.1 = (f32[32,256]{1,0:T(8,128)}, f32[32,256]{1,0:T(8,128)}, f32[32,256]{1,0:T(8,128)}) custom-call(f32[64,256]{1,0:T(8,128)} %bitcast.24, f32[1,64]{1,0:T(1,128)} %bitcast.26, f32[1,256]{1,0:T(1,128)} %bitcast.25, f32[32,256]{1,0:T(8,128)} %bitcast.22, f32[32,256]{1,0:T(8,128)} %bitcast.23), custom_call_target="tpu_custom_call" | custom-call | tf_op jit(solution)/shard_map/cg_step/pallas_call | solution.py:356
  46.1 0.0 copy-done
  46.1 0.0 copy-done.1
  46.1 0.0 copy-done.2
  46.1 1.4 %add_bitcast_fusion = (f32[256,32]{0,1:T(8,128)}, f32[256,32]{0,1:T(8,128)}, f32[256,32]{0,1:T(8,128)}) fusion(f32[32,256]{1,0:T(8,128)} %get-tuple-element.8, f32[256,32]{0,1:T(8,128)S(1)} %copy-done.1, f32[32,256]{1,0:T(8,128)} %get-tuple-element.6, f32[32,256]{1,0:T(8,128)} %get-tuple-element.7, f32[256,32]{0,1:T(8,128)S(1)} %copy-done, ...), kind=kLoop, calls=%fused_computation.2 | loop fusion | flops 49152 | bytes 294912 | tf_op jit(solution)/shard_map/transpose | solution.py:394
Async XLA Ops:
  0.6 45.4 %copy-start = (f32[256,32]{0,1:T(8,128)S(1)}, f32[256,32]{0,1:T(8,128)}, u32[]{:S(2)}) copy-start(f32[256,32]{0,1:T(8,128)} %param.10) | copy-start | bytes 98308
  0.6 45.4 %copy-start.1 = (f32[256,32]{0,1:T(8,128)S(1)}, f32[256,32]{0,1:T(8,128)}, u32[]{:S(2)}) copy-start(f32[256,32]{0,1:T(8,128)} %param.11) | copy-start | bytes 98308
  0.7 45.4 %copy-start.2 = (f32[256,32]{0,1:T(8,128)S(1)}, f32[256,32]{0,1:T(8,128)}, u32[]{:S(2)}) copy-start(f32[256,32]{0,1:T(8,128)} %param.9) | copy-start | bytes 98308
